TPU v7x, 256 devices: a whole 4x4x8 slice. The times are simulated.
256 devices in a mesh: lat: 8 (over x_hi, y), lon: 32 (over x_lo, z, core).
Axes of the slice: x: 4 (x_hi: 2, x_lo: 2; x = x_hi * 2 + x_lo), y: 4, z: 8, core: 2. Of those that a mesh axis runs over, the one named last changes fastest.
Arguments:
- inputs: bfloat16 [720, 1440, 256], P('lat', 'lon'), may hold values from -6 to 6
- kernel: bfloat16 [3, 3, 256, 256], replicated, may hold values from -0.125 to 0.125
- cotangent: bfloat16 [720, 1440, 256], P('lat', 'lon'), may hold values from -6 to 6
Outputs:
- outputs: bfloat16 [720, 1440, 256], P('lat', 'lon')
- input_grad: bfloat16 [720, 1440, 256], P('lat', 'lon')
- kernel_grad: float32 [3, 3, 256, 256], replicated
All inputs are finite; a program needn't handle non-finite values.
Results may differ from a plain program's by a relative error of at most 0.001.
Values may be sent and summed in bfloat16 or wider, within the bound.
A program may use at most 192 MiB of HBM per device.

v0:
```python
import math
import jax
import jax.numpy as jnp
from jax import lax
from jax.sharding import PartitionSpec as P


def with_halo(cells, sides, width):
    for axis, dim in sides:
        count = lax.axis_size(axis)
        head = lax.slice_in_dim(cells, 0, width, axis=dim)
        tail = lax.slice_in_dim(cells, cells.shape[dim] - width, cells.shape[dim], axis=dim)
        cells = jnp.concatenate(
            [
                lax.ppermute(tail, axis, [(i, (i + 1) % count) for i in range(count)]),
                cells,
                lax.ppermute(head, axis, [((i + 1) % count, i) for i in range(count)]),
            ],
            axis=dim,
        )
    return cells


def from_behind(value, axis, steps):
    count = lax.axis_size(axis)
    pairs = [(source, (source + steps) % count) for source in range(count)]
    return lax.ppermute(value, axis, pairs)


def patches(padded, rows, cols):
    pieces = [
        padded[row_tap : row_tap + rows, col_tap : col_tap + cols]
        for row_tap in range(3)
        for col_tap in range(3)
    ]
    return jnp.concatenate(pieces, axis=-1).reshape(rows * cols, -1)


def surround(field):
    return with_halo(field, (("lat", 0), ("lon", 1)), 1)


def polar(padded):
    both = jnp.stack([padded[1], padded[-2]])
    moved = from_behind(both, "lon", lax.axis_size("lon") // 2)
    return (moved[0], moved[1])


def edge_term(row_data, weights, cols, width):
    stacked = jnp.concatenate([row_data[offset : offset + cols] for offset in range(3)], axis=-1)
    return jnp.dot(stacked, weights.reshape(-1, width), preferred_element_type=jnp.float32)


def local(inputs, kernel, cotangent):
    rows, cols, width = inputs.shape
    north = lax.axis_index("lat") == 0
    south = lax.axis_index("lat") == lax.axis_size("lat") - 1
    padded = surround(inputs)
    top, bottom = polar(padded)
    padded = jnp.concatenate(
        [
            jnp.where(north, top, padded[0])[None],
            padded[1:-1],
            jnp.where(south, bottom, padded[-1])[None],
        ],
        0,
    )
    columns = patches(padded, rows, cols)
    outputs = jnp.dot(columns, kernel.reshape(-1, width), preferred_element_type=jnp.float32)
    outputs = outputs.reshape(rows, cols, width).astype(jnp.bfloat16)
    flat_grad = cotangent.reshape(-1, width)
    local_grad = lax.dot_general(
        columns, flat_grad, (((0,), (0,)), ((), ())), preferred_element_type=jnp.float32
    )
    local_grad = local_grad.reshape(3, 3, width, width)
    padded_grad = surround(cotangent)
    grad_top, grad_bottom = polar(padded_grad)
    empty_row = jnp.zeros_like(padded_grad[0])
    padded_grad = jnp.concatenate(
        [
            jnp.where(north, empty_row, padded_grad[0])[None],
            padded_grad[1:-1],
            jnp.where(south, empty_row, padded_grad[-1])[None],
        ],
        0,
    )
    flipped = jnp.transpose(kernel[::-1, ::-1], (0, 1, 3, 2))
    input_grad = jnp.dot(
        patches(padded_grad, rows, cols),
        flipped.reshape(-1, width),
        preferred_element_type=jnp.float32,
    )
    input_grad = input_grad.reshape(rows, cols, width)
    north_term = edge_term(grad_top, flipped[2], cols, width)
    south_term = edge_term(grad_bottom, flipped[0], cols, width)
    input_grad = input_grad.at[0].add(jnp.where(north, north_term, 0.0))
    input_grad = input_grad.at[-1].add(jnp.where(south, south_term, 0.0))
    factor = 1.0 / math.sqrt(rows * cols * lax.axis_size("lat") * lax.axis_size("lon"))
    summed = lax.psum(local_grad, ("lat", "lon"))
    return (outputs, input_grad.astype(jnp.bfloat16), summed * factor)


def solution(mesh):
    in_specs = (P("lat", "lon", None), P(), P("lat", "lon", None))
    out_specs = (P("lat", "lon", None), P("lat", "lon", None), P())
    return jax.shard_map(local, mesh=mesh, in_specs=in_specs, out_specs=out_specs, check_vma=False)
```

profile of v0, /device:TPU:2, one launch (start us, length us, event | category | flops | bytes accessed | tf_op | source)
XLA Modules:
  0.0 427.5 jit_solution(5525735376347575952)
XLA Ops:
  7.2 0.8 fusion.70
  8.0 4.6 %collective-permute-start.1 = (bf16[1,45,256]{2,1,0:T(8,128)(2,1)S(1)}, bf16[1,45,256]{2,1,0:T(8,128)(2,1)S(1)}, u32[]{:S(2)}, u32[]{:S(2)}) collective-permute-start(bf16[1,45,256]{2,1,0:T(8,128)(2,1)S(1)} %get-tuple-element.37), channel_id=1, source_target_pairs={{32,0},{64,32},{96,64},{128,96},{160,128},{192,160},{224,192},{0,2... | collective-permute-start | bytes 69128 | tf_op jit(solution)/shard_map/ppermute | solution.py:17
  12.6 1.4 fusion.69
  13.9 5.6 %collective-permute-start.6 = (bf16[1,45,256]{2,1,0:T(8,128)(2,1)}, bf16[1,45,256]{2,1,0:T(8,128)(2,1)S(1)}, u32[]{:S(2)}, u32[]{:S(2)}) collective-permute-start(bf16[1,45,256]{2,1,0:T(8,128)(2,1)} %get-tuple-element.35), channel_id=1, source_target_pairs={{32,0},{64,32},{96,64},{128,96},{160,128},{192,160},{224,192},{0,2... | collective-permute-start | bytes 69128 | tf_op jit(solution)/shard_map/ppermute | solution.py:17
  19.6 1.6 copy.6
  21.2 0.9 fusion.71
  22.2 1.1 rev.3
  23.3 1.9 reshape.103
  25.2 2.0 collective-permute-done.5
  27.4 0.1 fusion.67
  27.6 4.3 collective-permute-start.8
  32.1 0.1 fusion.68
  32.3 3.8 collective-permute-start.3
  36.2 1.1 collective-permute-start.9
  37.3 1.1 collective-permute-done.2
  38.5 1.7 collective-permute-start.4
  40.1 1.6 pad_maximum_fusion.1
  41.9 1.6 fusion.7
  43.5 2.9 fusion.5
  46.3 2.9 fusion.19
  49.3 2.8 fusion.18
  52.0 1.6 constant_dynamic-update-slice_fusion.7
  53.7 3.1 fusion.17
  56.7 1.7 fusion.3
  58.4 2.9 fusion.1
  61.3 2.9 fusion.16
  64.1 9.8 %fusion.72 = f32[90,45,256]{2,1,0:T(8,128)S(1)} fusion(bf16[90,45,2304]{2,1,0:T(8,128)(2,1)} %fusion.16, bf16[2304,256,1]{1,0,2:T(8,128)(2,1)S(1)} %bitcast.50), kind=kOutput, calls=%fused_computation.114 | convolution fusion | flops 4777574400 | bytes 23989248 | tf_op jit(solution)/shard_map/dot_general | solution.py:88
  74.0 1.6 pad_maximum_fusion
  75.8 0.8 copy-done.4
  76.6 0.2 fusion.62
  76.8 0.2 fusion.28
  77.0 1.6 convert_element_type.7
  78.6 1.6 fusion.15
  80.3 2.8 fusion.13
  83.1 2.9 fusion.23
  86.0 2.8 fusion.22
  88.8 1.6 constant_dynamic-update-slice_fusion.3
  90.4 3.1 fusion.21
  93.5 1.7 fusion.11
  95.2 2.8 fusion.9
  98.0 2.8 fusion.20
  100.8 19.4 %reshape.99 = bf16[4050,2304]{1,0:T(8,128)(2,1)} reshape(bf16[90,45,2304]{2,1,0:T(8,128)(2,1)} %fusion.20) | data formatting | bytes 37324800 | tf_op jit(solution)/shard_map/reshape | solution.py:36
  120.2 25.0 %copy.7 = bf16[4050,2304]{0,1:T(8,128)(2,1)} copy(bf16[4050,2304]{1,0:T(8,128)(2,1)} %reshape.99) | data formatting | bytes 37324800 | tf_op jit(solution)/shard_map/reshape | solution.py:36
  145.1 10.6 %fusion.24 = f32[3,3,256,256]{3,2,1,0:T(8,128)} fusion(bf16[3,3,256,4050]{3,2,1,0:T(8,128)(2,1)} %bitcast.46, bf16[4050,256,1,1]{1,0,2,3:T(8,128)(2,1)S(1)} %copy-done.2), kind=kOutput, calls=%fused_computation.42 | convolution fusion | flops 4777574400 | bytes 23095296 | tf_op jit(solution)/shard_map/dot_general | solution.py:72
  155.7 1.2 copy-done.5
  157.0 11.5 %convolution_convert_fusion = bf16[90,45,256]{2,1,0:T(8,128)(2,1)} fusion(bf16[90,45,2304]{2,1,0:T(8,128)(2,1)} %fusion.20, bf16[2304,256,1]{1,0,2:T(8,128)(2,1)S(1)} %bitcast.49), kind=kOutput, calls=%fused_computation.44 | convolution fusion | flops 4778611200 | bytes 21915648 | tf_op jit(solution)/shard_map/dot_general | solution.py:69
  168.5 248.7 %all-reduce.2.cloned.1.call-done = f32[3,3,256,256]{3,2,1,0:T(8,128)} async-done(((f32[3,3,256,256]{3,2,1,0:T(8,128)}), f32[3,3,256,256]{3,2,1,0:T(8,128)}) %all-reduce.2.cloned.1.call-update) | async-done | bytes 2359312 | tf_op jit(solution)/shard_map/psum | solution.py:99
  417.2 3.3 broadcast_multiply_fusion
  (40 shorter events, 1.1 us)
Async XLA Ops:
  7.2 410.0 %all-reduce.2.cloned.1.call-start = ((), (), s32[]{:S(2)}) async-start(), calls=%async_computation | async-start | bytes 4718592 | tf_op jit(solution)/shard_map/psum | solution.py:99
  8.0 24.1 %collective-permute-start.1 = (bf16[1,45,256]{2,1,0:T(8,128)(2,1)S(1)}, bf16[1,45,256]{2,1,0:T(8,128)(2,1)S(1)}, u32[]{:S(2)}, u32[]{:S(2)}) collective-permute-start(bf16[1,45,256]{2,1,0:T(8,128)(2,1)S(1)} %get-tuple-element.37), channel_id=1, source_target_pairs={{32,0},{64,32},{96,64},{128,96},{160,128},{192,160},{224,192},{0,2... | collective-permute-start | bytes 69128 | tf_op jit(solution)/shard_map/ppermute | solution.py:17
  12.5 19.3 %collective-permute-start = (bf16[1,45,256]{2,1,0:T(8,128)(2,1)S(1)}, bf16[1,45,256]{2,1,0:T(8,128)(2,1)S(1)}, u32[]{:S(2)}, u32[]{:S(2)}) collective-permute-start(bf16[1,45,256]{2,1,0:T(8,128)(2,1)S(1)} %get-tuple-element.38), channel_id=1, source_target_pairs={{0,32},{32,64},{64,96},{96,128},{128,160},{160,192},{192,224},{224... | collective-permute-start | bytes 69128 | tf_op jit(solution)/shard_map/ppermute | solution.py:15
  13.9 13.4 %collective-permute-start.6 = (bf16[1,45,256]{2,1,0:T(8,128)(2,1)}, bf16[1,45,256]{2,1,0:T(8,128)(2,1)S(1)}, u32[]{:S(2)}, u32[]{:S(2)}) collective-permute-start(bf16[1,45,256]{2,1,0:T(8,128)(2,1)} %get-tuple-element.35), channel_id=1, source_target_pairs={{32,0},{64,32},{96,64},{128,96},{160,128},{192,160},{224,192},{0,2... | collective-permute-start | bytes 69128 | tf_op jit(solution)/shard_map/ppermute | solution.py:17
  19.6 7.7 %collective-permute-start.5 = (bf16[1,45,256]{2,1,0:T(8,128)(2,1)}, bf16[1,45,256]{2,1,0:T(8,128)(2,1)S(1)}, u32[]{:S(2)}, u32[]{:S(2)}) collective-permute-start(bf16[1,45,256]{2,1,0:T(8,128)(2,1)} %get-tuple-element.36), channel_id=1, source_target_pairs={{0,32},{32,64},{64,96},{96,128},{128,160},{160,192},{192,224},{224... | collective-permute-start | bytes 69128 | tf_op jit(solution)/shard_map/ppermute | solution.py:15
  21.2 2.0 copy-start
  27.2 4.7 %copy-start.1 = (bf16[90,45,256]{2,1,0:T(8,128)(2,1)S(1)}, bf16[90,45,256]{2,1,0:T(8,128)(2,1)}, u32[]{:S(2)}) copy-start(bf16[90,45,256]{2,1,0:T(8,128)(2,1)} %param.7) | copy-start | bytes 6220804
  27.5 8.6 %collective-permute-start.7 = (bf16[92,1,256]{2,1,0:T(2,128)(2,1)S(1)}, bf16[92,1,256]{2,1,0:T(2,128)(2,1)S(1)}, u32[]{:S(2)}, u32[]{:S(2)}) collective-permute-start(bf16[92,1,256]{2,1,0:T(2,128)(2,1)S(1)} %get-tuple-element.31), channel_id=1, source_target_pairs={{0,1},{1,2},{2,3},{3,4},{4,5},{5,6},{6,7},{7,8},{8,9},{9,10},{10,1... | collective-permute-start | bytes 141320 | tf_op jit(solution)/shard_map/ppermute | solution.py:15
  27.6 8.5 %collective-permute-start.8 = (bf16[92,1,256]{2,1,0:T(2,128)(2,1)S(1)}, bf16[92,1,256]{2,1,0:T(2,128)(2,1)S(1)}, u32[]{:S(2)}, u32[]{:S(2)}) collective-permute-start(bf16[92,1,256]{2,1,0:T(2,128)(2,1)S(1)} %get-tuple-element.32), channel_id=1, source_target_pairs={{1,0},{2,1},{3,2},{4,3},{5,4},{6,5},{7,6},{8,7},{9,8},{10,9},{11,1... | collective-permute-start | bytes 141320 | tf_op jit(solution)/shard_map/ppermute | solution.py:17
  32.2 6.2 %collective-permute-start.2 = (bf16[92,1,256]{2,1,0:T(2,128)(2,1)S(1)}, bf16[92,1,256]{2,1,0:T(2,128)(2,1)S(1)}, u32[]{:S(2)}, u32[]{:S(2)}) collective-permute-start(bf16[92,1,256]{2,1,0:T(2,128)(2,1)S(1)} %get-tuple-element.33), channel_id=1, source_target_pairs={{0,1},{1,2},{2,3},{3,4},{4,5},{5,6},{6,7},{7,8},{8,9},{9,10},{10,1... | collective-permute-start | bytes 141320 | tf_op jit(solution)/shard_map/ppermute | solution.py:15
  32.3 6.1 %collective-permute-start.3 = (bf16[92,1,256]{2,1,0:T(2,128)(2,1)S(1)}, bf16[92,1,256]{2,1,0:T(2,128)(2,1)S(1)}, u32[]{:S(2)}, u32[]{:S(2)}) collective-permute-start(bf16[92,1,256]{2,1,0:T(2,128)(2,1)S(1)} %get-tuple-element.34), channel_id=1, source_target_pairs={{1,0},{2,1},{3,2},{4,3},{5,4},{6,5},{7,6},{8,7},{9,8},{10,9},{11,1... | collective-permute-start | bytes 141320 | tf_op jit(solution)/shard_map/ppermute | solution.py:17
  36.2 39.5 %collective-permute-start.9 = (bf16[2,47,256]{2,1,0:T(8,128)(2,1)S(1)}, bf16[2,47,256]{2,1,0:T(8,128)(2,1)S(1)}, u32[]{:S(2)}, u32[]{:S(2)}) collective-permute-start(bf16[2,47,256]{2,1,0:T(8,128)(2,1)S(1)} %fusion.57), channel_id=1, source_target_pairs={{0,16},{1,17},{2,18},{3,19},{4,20},{5,21},{6,22},{7,23},{8,24},{9,... | collective-permute-start | bytes 144392 | tf_op jit(solution)/shard_map/ppermute | solution.py:27
  38.5 40.2 %collective-permute-start.4 = (bf16[2,47,256]{2,1,0:T(8,128)(2,1)S(1)}, bf16[2,47,256]{2,1,0:T(8,128)(2,1)S(1)}, u32[]{:S(2)}, u32[]{:S(2)}) collective-permute-start(bf16[2,47,256]{2,1,0:T(8,128)(2,1)S(1)} %fusion.54), channel_id=1, source_target_pairs={{0,16},{1,17},{2,18},{3,19},{4,20},{5,21},{6,22},{7,23},{8,24},{9,... | collective-permute-start | bytes 144392 | tf_op jit(solution)/shard_map/ppermute | solution.py:27
  61.3 2.9 copy-start.6
  75.6 1.0 copy-start.4
  75.6 1.2 copy-start.3
  120.2 25.0 %copy-start.2 = (bf16[4050,256,1,1]{1,0,2,3:T(8,128)(2,1)S(1)}, bf16[4050,256,1,1]{1,0,2,3:T(8,128)(2,1)}, u32[]{:S(2)}) copy-start(bf16[4050,256,1,1]{1,0,2,3:T(8,128)(2,1)} %reshape.103) | copy-start | bytes 6220804
  155.7 1.3 copy-start.5
Sparse Core Ops, SparseCore 0:
  155.9 261.2 all-reduce.1
where the time goes:
time: 435 us; the launch traced here: 428 us
  waiting for transfers between devices  252 us (58%)
  local copies, waits for them, and re-layouts  58.2 us (13%)
  other arithmetic  49.3 us (11%)
  matrix products  32.3 us (7%)
  starting transfers between devices  21.3 us (5%)
  between operations  14.5 us (3%)
    psum x1, waiting for transfers between devices, local(): summed = lax.psum(local_grad, ('lat', 'lon'))  249 us
    reshape x2, local copies, waits for them, and re-layouts, patches(): return jnp.concatenate(pieces, axis=-1).reshape(rows * cols, -1)  44.3 us
    unnamed x14, other arithmetic  35.5 us
    ppermute x4, starting transfers between devices, with_halo(): lax.ppermute(head, axis, [((i + 1) % count, i) for i in range(count)])  18.3 us
    dot_general x1, matrix products, local(): jnp.dot(columns, kernel.reshape(-1, width), preferred_element_type=jnp.fl...  11.5 us
    dot_general x1, matrix products, local(): lax.dot_general(columns, flat_grad, (((0,), (0,)), ((), ())), preferred_e...  10.6 us
    dot_general x1, matrix products, local(): jnp.dot(patches(padded_grad, rows, cols), flipped.reshape(-1, width), pre...  9.85 us
  transfers between devices with their start and end apart: 11, of which 3 were waited for; matrix products, arithmetic and copies ran while one was open for 13% of the time, Pallas kernels for 0%

commit v1 on v0

--- a/solution.py
+++ b/solution.py
@@ -96,7 +96,7 @@
     input_grad = input_grad.at[0].add(jnp.where(north, north_term, 0.0))
     input_grad = input_grad.at[-1].add(jnp.where(south, south_term, 0.0))
     factor = 1.0 / math.sqrt(rows * cols * lax.axis_size("lat") * lax.axis_size("lon"))
-    summed = lax.psum(local_grad, ("lat", "lon"))
+    summed = lax.psum(lax.psum(local_grad, "lon"), "lat")
     return (outputs, input_grad.astype(jnp.bfloat16), summed * factor)
 
 

time: 435 us -> 464 us (1.067)
  waiting for transfers between devices: 252 us -> 275 us
    psum x1 -> x2, waiting for transfers between devices: 249 us -> 271 us  [local(): summed = lax.psum(lax.psum(local_grad, 'lon'), 'lat')]
  transfers between devices with their start and end apart: 11 -> 12, of which waited for: 3 -> 5; matrix products, arithmetic and copies ran while one was open for 13% -> 14% of each run, Pallas kernels for 0% -> 0%
where the time goes in v1:
time: 464 us; the launch traced here: 458 us
  waiting for transfers between devices  275 us (59%)
  local copies, waits for them, and re-layouts  62.3 us (13%)
  other arithmetic  52.2 us (11%)
  matrix products  32.4 us (7%)
  starting transfers between devices  20.7 us (4%)
  between operations  14.5 us (3%)
    psum x2, waiting for transfers between devices, local(): summed = lax.psum(lax.psum(local_grad, 'lon'), 'lat')  271 us
    reshape x2, local copies, waits for them, and re-layouts, patches(): return jnp.concatenate(pieces, axis=-1).reshape(rows * cols, -1)  44.2 us
    unnamed x14, other arithmetic  35.8 us
    ppermute x4, starting transfers between devices, with_halo(): lax.ppermute(head, axis, [((i + 1) % count, i) for i in range(count)])  18.9 us
    dot_general x1, matrix products, local(): jnp.dot(columns, kernel.reshape(-1, width), preferred_element_type=jnp.fl...  11.6 us
    dot_general x1, matrix products, local(): lax.dot_general(columns, flat_grad, (((0,), (0,)), ((), ())), preferred_e...  10.6 us
    dot_general x1, matrix products, local(): jnp.dot(patches(padded_grad, rows, cols), flipped.reshape(-1, width), pre...  9.83 us
  transfers between devices with their start and end apart: 12, of which 5 were waited for; matrix products, arithmetic and copies ran while one was open for 14% of the time, Pallas kernels for 0%

profile of v1, /device:TPU:2, one launch (start us, length us, event | category | flops | bytes accessed | tf_op | source)
XLA Modules:
  0.0 457.6 jit_solution(2365952053338268052)
XLA Ops:
  7.2 1.4 fusion.70
  8.6 4.6 collective-permute-start.1
  13.2 1.4 fusion.69
  14.5 5.6 %collective-permute-start.6 = (bf16[1,45,256]{2,1,0:T(8,128)(2,1)S(1)}, bf16[1,45,256]{2,1,0:T(8,128)(2,1)S(1)}, u32[]{:S(2)}, u32[]{:S(2)}) collective-permute-start(bf16[1,45,256]{2,1,0:T(8,128)(2,1)S(1)} %get-tuple-element.35), channel_id=1, source_target_pairs={{32,0},{64,32},{96,64},{128,96},{160,128},{192,160},{224,192},{0,2... | collective-permute-start | bytes 69128 | tf_op jit(solution)/shard_map/ppermute | solution.py:17
  20.2 1.7 copy.6
  21.9 1.1 reverse_bitcast_fusion
  23.0 1.9 reshape.103
  24.9 1.9 constant_dynamic-update-slice_fusion.1
  27.0 0.8 collective-permute-done.5
  28.1 4.8 %collective-permute-start.3 = (bf16[92,1,256]{2,1,0:T(2,128)(2,1)S(1)}, bf16[92,1,256]{2,1,0:T(2,128)(2,1)S(1)}, u32[]{:S(2)}, u32[]{:S(2)}) collective-permute-start(bf16[92,1,256]{2,1,0:T(2,128)(2,1)S(1)} %get-tuple-element.34), channel_id=1, source_target_pairs={{1,0},{2,1},{3,2},{4,3},{5,4},{6,5},{7,6},{8,7},{9,8},{10,9},{11,1... | collective-permute-start | bytes 141320 | tf_op jit(solution)/shard_map/ppermute | solution.py:17
  32.9 2.2 collective-permute-done.2
  35.1 1.0 collective-permute-start.4
  36.0 1.6 pad_maximum_fusion
  37.7 1.8 collective-permute-done.4
  39.6 1.7 fusion.15
  41.2 2.8 fusion.13
  44.1 2.8 fusion.23
  46.9 2.9 fusion.22
  49.8 1.7 constant_dynamic-update-slice_fusion.3
  51.5 3.0 fusion.21
  54.5 1.7 fusion.11
  56.2 2.9 fusion.9
  59.1 2.7 fusion.20
  61.8 19.9 %reshape.99 = bf16[4050,2304]{1,0:T(8,128)(2,1)} reshape(bf16[90,45,2304]{2,1,0:T(8,128)(2,1)} %fusion.20) | data formatting | bytes 37324800 | tf_op jit(solution)/shard_map/reshape | solution.py:36
  81.7 24.3 %copy.7 = bf16[4050,2304]{0,1:T(8,128)(2,1)} copy(bf16[4050,2304]{1,0:T(8,128)(2,1)} %reshape.99) | data formatting | bytes 37324800 | tf_op jit(solution)/shard_map/reshape | solution.py:36
  106.0 10.6 %fusion.24 = f32[3,3,256,256]{3,2,1,0:T(8,128)} fusion(bf16[3,3,256,4050]{3,2,1,0:T(8,128)(2,1)} %bitcast.46, bf16[4050,256,1,1]{1,0,2,3:T(8,128)(2,1)} %reshape.103), kind=kOutput, calls=%fused_computation.42 | convolution fusion | flops 4777574400 | bytes 23095296 | tf_op jit(solution)/shard_map/dot_general | solution.py:72
  116.7 0.8 fusion.67
  117.5 3.9 collective-permute-start.8
  121.4 2.0 fusion.71
  123.4 1.1 rev.3
  124.5 1.3 fusion.57
  126.6 2.3 pad_maximum_fusion.1
  129.7 1.6 fusion.7
  131.3 2.7 fusion.5
  134.1 2.8 fusion.19
  136.8 3.6 fusion.18
  140.5 1.5 constant_dynamic-update-slice_fusion.7
  142.0 2.9 fusion.17
  144.9 1.6 fusion.3
  146.5 2.7 fusion.1
  149.3 2.8 fusion.16
  152.1 194.2 %all-reduce.3.cloned.1.call-done = f32[3,3,256,256]{3,2,1,0:T(8,128)} async-done(((f32[3,3,256,256]{3,2,1,0:T(8,128)}), f32[3,3,256,256]{3,2,1,0:T(8,128)}) %all-reduce.3.cloned.1.call-update) | async-done | bytes 2359312 | tf_op jit(solution)/shard_map/psum | solution.py:99
  346.3 9.8 %fusion.72 = f32[90,45,256]{2,1,0:T(8,128)S(1)} fusion(bf16[90,45,2304]{2,1,0:T(8,128)(2,1)} %fusion.16, bf16[2304,256,1]{1,0,2:T(8,128)(2,1)S(1)} %bitcast.50), kind=kOutput, calls=%fused_computation.114 | convolution fusion | flops 4777574400 | bytes 23989248 | tf_op jit(solution)/shard_map/dot_general | solution.py:88
  356.1 0.9 slice_bitcast_fusion.2
  357.5 1.6 convert_element_type.7
  359.1 11.6 %convolution_convert_fusion = bf16[90,45,256]{2,1,0:T(8,128)(2,1)} fusion(bf16[90,45,2304]{2,1,0:T(8,128)(2,1)} %fusion.20, bf16[2304,256,1]{1,0,2:T(8,128)(2,1)S(1)} %bitcast.49), kind=kOutput, calls=%fused_computation.44 | convolution fusion | flops 4778611200 | bytes 21915648 | tf_op jit(solution)/shard_map/dot_general | solution.py:69
  370.7 76.5 %all-reduce.5.cloned.1.call-done = f32[3,3,256,256]{3,2,1,0:T(8,128)} async-done(((f32[3,3,256,256]{3,2,1,0:T(8,128)}), f32[3,3,256,256]{3,2,1,0:T(8,128)}) %all-reduce.5.cloned.1.call-update) | async-done | bytes 2359312 | tf_op jit(solution)/shard_map/psum | solution.py:99
  447.2 3.3 broadcast_multiply_fusion
  (45 shorter events, 2.7 us)
Async XLA Ops:
  7.2 339.1 %all-reduce.3.cloned.1.call-start = ((), (), s32[]{:S(2)}) async-start(), calls=%async_computation | async-start | bytes 4718592 | tf_op jit(solution)/shard_map/psum | solution.py:99
  8.6 18.3 %collective-permute-start.1 = (bf16[1,45,256]{2,1,0:T(8,128)(2,1)S(1)}, bf16[1,45,256]{2,1,0:T(8,128)(2,1)S(1)}, u32[]{:S(2)}, u32[]{:S(2)}) collective-permute-start(bf16[1,45,256]{2,1,0:T(8,128)(2,1)S(1)} %get-tuple-element.37), channel_id=1, source_target_pairs={{32,0},{64,32},{96,64},{128,96},{160,128},{192,160},{224,192},{0,2... | collective-permute-start | bytes 69128 | tf_op jit(solution)/shard_map/ppermute | solution.py:17
  13.2 11.8 %collective-permute-start = (bf16[1,45,256]{2,1,0:T(8,128)(2,1)}, bf16[1,45,256]{2,1,0:T(8,128)(2,1)S(1)}, u32[]{:S(2)}, u32[]{:S(2)}) collective-permute-start(bf16[1,45,256]{2,1,0:T(8,128)(2,1)} %get-tuple-element.38), channel_id=1, source_target_pairs={{0,32},{32,64},{64,96},{96,128},{128,160},{160,192},{192,224},{224... | collective-permute-start | bytes 69128 | tf_op jit(solution)/shard_map/ppermute | solution.py:15
  14.5 18.3 %collective-permute-start.6 = (bf16[1,45,256]{2,1,0:T(8,128)(2,1)S(1)}, bf16[1,45,256]{2,1,0:T(8,128)(2,1)S(1)}, u32[]{:S(2)}, u32[]{:S(2)}) collective-permute-start(bf16[1,45,256]{2,1,0:T(8,128)(2,1)S(1)} %get-tuple-element.35), channel_id=1, source_target_pairs={{32,0},{64,32},{96,64},{128,96},{160,128},{192,160},{224,192},{0,2... | collective-permute-start | bytes 69128 | tf_op jit(solution)/shard_map/ppermute | solution.py:17
  20.2 2.8 copy-start
  20.2 7.7 %collective-permute-start.5 = (bf16[1,45,256]{2,1,0:T(8,128)(2,1)}, bf16[1,45,256]{2,1,0:T(8,128)(2,1)S(1)}, u32[]{:S(2)}, u32[]{:S(2)}) collective-permute-start(bf16[1,45,256]{2,1,0:T(8,128)(2,1)} %get-tuple-element.36), channel_id=1, source_target_pairs={{0,32},{32,64},{64,96},{96,128},{128,160},{160,192},{192,224},{224... | collective-permute-start | bytes 69128 | tf_op jit(solution)/shard_map/ppermute | solution.py:15
  24.9 2.9 copy-start.1
  28.0 7.1 %collective-permute-start.2 = (bf16[92,1,256]{2,1,0:T(2,128)(2,1)S(1)}, bf16[92,1,256]{2,1,0:T(2,128)(2,1)S(1)}, u32[]{:S(2)}, u32[]{:S(2)}) collective-permute-start(bf16[92,1,256]{2,1,0:T(2,128)(2,1)S(1)} %get-tuple-element.33), channel_id=1, source_target_pairs={{0,1},{1,2},{2,3},{3,4},{4,5},{5,6},{6,7},{7,8},{8,9},{9,10},{10,1... | collective-permute-start | bytes 141320 | tf_op jit(solution)/shard_map/ppermute | solution.py:15
  28.1 7.0 %collective-permute-start.3 = (bf16[92,1,256]{2,1,0:T(2,128)(2,1)S(1)}, bf16[92,1,256]{2,1,0:T(2,128)(2,1)S(1)}, u32[]{:S(2)}, u32[]{:S(2)}) collective-permute-start(bf16[92,1,256]{2,1,0:T(2,128)(2,1)S(1)} %get-tuple-element.34), channel_id=1, source_target_pairs={{1,0},{2,1},{3,2},{4,3},{5,4},{6,5},{7,6},{8,7},{9,8},{10,9},{11,1... | collective-permute-start | bytes 141320 | tf_op jit(solution)/shard_map/ppermute | solution.py:17
  35.1 4.5 collective-permute-start.4
  46.9 2.9 copy-start.3
  116.6 330.6 %all-reduce.5.cloned.1.call-start = ((), (), s32[]{:S(2)}) async-start(), calls=%async_computation.1 | async-start | bytes 4718592 | tf_op jit(solution)/shard_map/psum | solution.py:99
  117.5 7.0 %collective-permute-start.7 = (bf16[92,1,256]{2,1,0:T(2,128)(2,1)}, bf16[92,1,256]{2,1,0:T(2,128)(2,1)}, u32[]{:S(2)}, u32[]{:S(2)}) collective-permute-start(bf16[92,1,256]{2,1,0:T(2,128)(2,1)} %get-tuple-element.31), channel_id=1, source_target_pairs={{0,1},{1,2},{2,3},{3,4},{4,5},{5,6},{6,7},{7,8},{8,9},{9,10},{10,1... | collective-permute-start | bytes 141320 | tf_op jit(solution)/shard_map/ppermute | solution.py:15
  117.5 7.0 %collective-permute-start.8 = (bf16[92,1,256]{2,1,0:T(2,128)(2,1)}, bf16[92,1,256]{2,1,0:T(2,128)(2,1)S(1)}, u32[]{:S(2)}, u32[]{:S(2)}) collective-permute-start(bf16[92,1,256]{2,1,0:T(2,128)(2,1)} %get-tuple-element.32), channel_id=1, source_target_pairs={{1,0},{2,1},{3,2},{4,3},{5,4},{6,5},{7,6},{8,7},{9,8},{10,9},{11,1... | collective-permute-start | bytes 141320 | tf_op jit(solution)/shard_map/ppermute | solution.py:17
  125.8 230.3 %collective-permute-start.9 = (bf16[2,47,256]{2,1,0:T(8,128)(2,1)}, bf16[2,47,256]{2,1,0:T(8,128)(2,1)}, u32[]{:S(2)}, u32[]{:S(2)}) collective-permute-start(bf16[2,47,256]{2,1,0:T(8,128)(2,1)} %fusion.57), channel_id=1, source_target_pairs={{0,16},{1,17},{2,18},{3,19},{4,20},{5,21},{6,22},{7,23},{8,24},{9,... | collective-permute-start | bytes 144392 | tf_op jit(solution)/shard_map/ppermute | solution.py:27
  136.8 3.6 copy-start.2
  152.1 194.2 %copy-start.7 = (bf16[3,3,256,256]{2,3,1,0:T(8,128)(2,1)S(1)}, bf16[3,3,256,256]{2,3,1,0:T(8,128)(2,1)}, u32[]{:S(2)}) copy-start(bf16[3,3,256,256]{2,3,1,0:T(8,128)(2,1)} %rev.3) | copy-start | bytes 3538948
  346.3 10.8 %copy-start.5 = (bf16[1,3,256,256]{3,2,1,0:T(8,128)(2,1)S(1)}, bf16[1,3,256,256]{3,2,1,0:T(8,128)(2,1)}, u32[]{:S(2)}) copy-start(bf16[1,3,256,256]{3,2,1,0:T(8,128)(2,1)} %get-tuple-element.40) | copy-start | bytes 1179652
  346.3 11.0 %copy-start.4 = (bf16[1,3,256,256]{3,2,1,0:T(8,128)(2,1)S(1)}, bf16[1,3,256,256]{3,2,1,0:T(8,128)(2,1)}, u32[]{:S(2)}) copy-start(bf16[1,3,256,256]{3,2,1,0:T(8,128)(2,1)} %get-tuple-element.39) | copy-start | bytes 1179652
  357.5 1.6 copy-start.6
Sparse Core Ops, SparseCore 0:
  116.7 229.4 all-reduce.2
  348.9 98.2 all-reduce.4
